TPU v7x, 32 devices: a whole 2x2x4 slice. The times are simulated.
32 devices in a mesh: grp: 2 (over y), blk: 8 (over z, x), seq: 2 (over core).
Axes of the slice: x: 2, y: 2, z: 4, core: 2. Of those that a mesh axis runs over, the one named last changes fastest.
Arguments:
- image_qkv: bfloat16 [4096, 4608], P(('grp', 'blk', 'seq')), parts along dimension 0, may hold values from -6 to 6
- image_qkv_tangent: bfloat16 [4096, 4608], P(('grp', 'blk', 'seq')), parts along dimension 0, may hold values from -6 to 6
- text_kv: bfloat16 [1024, 3072], P(('grp', 'blk', 'seq')), parts along dimension 0, may hold values from -6 to 6
- text_kv_tangent: bfloat16 [1024, 3072], P(('grp', 'blk', 'seq')), parts along dimension 0, may hold values from -6 to 6
- out_weight: bfloat16 [1536, 3072], P(None, ('blk', 'seq')), may hold values from -0.15625 to 0.15625
- gate_table: float32 [64, 3072], replicated, may hold values from -6 to 6
- timesteps: int32 [16], P(('grp', 'blk')), parts along dimension 0, may hold values from 0 to 63
- image_lengths: int32 [16], P(('grp', 'blk')), parts along dimension 0, may hold values from 128 to 256, as said below
- text_lengths: int32 [16], P(('grp', 'blk')), parts along dimension 0, may hold values from 16 to 64, as said below
Outputs:
- output: bfloat16 [4096, 3072], P(('grp', 'blk', 'seq')), parts along dimension 0
- output_tangent: bfloat16 [4096, 3072], P(('grp', 'blk', 'seq')), parts along dimension 0
There are 2 independent parts, one for each index of `grp`. A program takes and returns all parts, laid end to end along the dimension named above; an argument that names none is the same for every part. Nothing has to cross between parts.
Inputs may be any that keep to these rules, and one draw needn't show every extreme that they name: `image_lengths`: the first that many of an image's 256 image slots are live; some image has all of them live. `text_lengths`: the first that many of an image's 64 text slots are live; some image has all of them live.
All inputs are finite; a program needn't handle non-finite values.
Results may differ from a plain program's by a relative error of at most 0.0059.
Values may be sent and summed in bfloat16 or wider, within the bound.
A program may use at most 128 MiB of HBM per device.

v0:
```python
import jax
import jax.numpy as jnp
from jax import lax
from jax.sharding import PartitionSpec as P

HS = 128
HEADS = 12


def attend(queries, tangent_queries, all_keys, tangent_keys, all_values, tangent_values, usable):
    factor = HS ** (-0.5)
    scores = (
        jnp.einsum("qhd,khd->hqk", queries, all_keys, preferred_element_type=jnp.float32) * factor
    )
    tangent_scores = (
        jnp.einsum("qhd,khd->hqk", tangent_queries, all_keys, preferred_element_type=jnp.float32)
        + jnp.einsum("qhd,khd->hqk", queries, tangent_keys, preferred_element_type=jnp.float32)
    ) * factor
    masked = jnp.where(usable[None, None, :], scores, -1e30)
    highest = jnp.max(masked, axis=-1, keepdims=True)
    raised = jnp.where(usable[None, None, :], jnp.exp(masked - highest), 0.0)
    weights = raised / jnp.sum(raised, axis=-1, keepdims=True)
    probs = weights.astype(jnp.bfloat16)
    centred = tangent_scores - jnp.sum(weights * tangent_scores, axis=-1, keepdims=True)
    tangent_probs = (weights * centred).astype(jnp.bfloat16)
    attended = jnp.einsum("hqk,khd->qhd", probs, all_values, preferred_element_type=jnp.float32)
    tangent_attended = jnp.einsum(
        "hqk,khd->qhd", tangent_probs, all_values, preferred_element_type=jnp.float32
    ) + jnp.einsum("hqk,khd->qhd", probs, tangent_values, preferred_element_type=jnp.float32)
    return (attended.astype(jnp.bfloat16), tangent_attended.astype(jnp.bfloat16))


def column_projector(stacked_rows, shard_piece):
    return jnp.dot(stacked_rows, shard_piece, preferred_element_type=jnp.float32)


def body(
    image_qkv,
    image_qkv_tangent,
    text_kv,
    text_kv_tangent,
    out_weight,
    gate_table,
    timesteps,
    image_lengths,
    text_lengths,
):
    row_count = image_qkv.shape[0]
    text_count = text_kv.shape[0]
    seq_count = lax.axis_size("seq")
    local_heads = HEADS // seq_count
    image_primal = image_qkv.reshape(row_count, 3, seq_count, local_heads, HS)
    image_tangent = image_qkv_tangent.reshape(row_count, 3, seq_count, local_heads, HS)
    text_primal = text_kv.reshape(text_count, 2, seq_count, local_heads, HS)
    text_tangent = text_kv_tangent.reshape(text_count, 2, seq_count, local_heads, HS)
    image_live = image_lengths[0]
    text_live = text_lengths[0]
    primal = lax.all_to_all(image_primal, "seq", split_axis=2, concat_axis=0, tiled=True)[:, :, 0]
    tangent = lax.all_to_all(image_tangent, "seq", split_axis=2, concat_axis=0, tiled=True)[:, :, 0]
    text_part = lax.all_to_all(text_primal, "seq", split_axis=2, concat_axis=0, tiled=True)[:, :, 0]
    text_tan = lax.all_to_all(text_tangent, "seq", split_axis=2, concat_axis=0, tiled=True)[:, :, 0]
    usable = jnp.concatenate(
        [
            jnp.arange(text_part.shape[0], dtype=jnp.int32) < text_live,
            jnp.arange(primal.shape[0], dtype=jnp.int32) < image_live,
        ],
        axis=0,
    )
    all_keys = jnp.concatenate([text_part[:, 0], primal[:, 1]], axis=0)
    tangent_keys = jnp.concatenate([text_tan[:, 0], tangent[:, 1]], axis=0)
    all_values = jnp.concatenate([text_part[:, 1], primal[:, 2]], axis=0)
    tangent_values = jnp.concatenate([text_tan[:, 1], tangent[:, 2]], axis=0)
    attended, tangent_attended = attend(
        primal[:, 0], tangent[:, 0], all_keys, tangent_keys, all_values, tangent_values, usable
    )
    gate_row = lax.dynamic_index_in_dim(gate_table, timesteps[0], 0, keepdims=False)
    local_primal, local_tangent = (
        lax.all_to_all(attended, "seq", split_axis=0, concat_axis=1, tiled=True),
        lax.all_to_all(tangent_attended, "seq", split_axis=0, concat_axis=1, tiled=True),
    )
    stacked_rows = jnp.concatenate(
        [local_primal.reshape(row_count, HEADS * HS), local_tangent.reshape(row_count, HEADS * HS)],
        axis=0,
    )
    projected = column_projector(
        stacked_rows, lax.all_gather(out_weight, ("blk", "seq"), axis=1, tiled=True)
    )
    output = (projected[:row_count] * gate_row).astype(jnp.bfloat16)
    output_tangent = (projected[row_count:] * gate_row).astype(jnp.bfloat16)
    return (output, output_tangent)


def solution(mesh):
    in_specs = (
        P(("grp", "blk", "seq"), None),
        P(("grp", "blk", "seq"), None),
        P(("grp", "blk", "seq"), None),
        P(("grp", "blk", "seq"), None),
        P(None, ("blk", "seq")),
        P(),
        P(("grp", "blk")),
        P(("grp", "blk")),
        P(("grp", "blk")),
    )
    out_specs = (P(("grp", "blk", "seq"), None), P(("grp", "blk", "seq"), None))
    return jax.shard_map(body, mesh=mesh, in_specs=in_specs, out_specs=out_specs, check_vma=False)
```

profile of v0, /device:TPU:1, one launch (start us, length us, event | category | flops | bytes accessed | tf_op | source)
XLA Modules:
  0.0 107.8 jit_solution(14306786214401964614)
XLA Ops:
  7.9 1.7 %copy.37 = bf16[128,4608]{0,1:T(8,128)(2,1)S(1)} copy(bf16[128,4608]{1,0:T(8,128)(2,1)} %param.9) | data formatting | bytes 2359296 | tf_op args[0]
  9.6 1.1 %copy.38 = bf16[128,3,2,6,128]{0,4,3,1,2:T(8,128)(2,1)} copy(bf16[128,3,2,6,128]{0,4,3,2,1:T(8,128)(2,1)S(1)} %bitcast.90) | data formatting | bytes 2359296 | tf_op jit(solution)/shard_map/reshape | solution.py:52
  10.8 3.6 %all-to-all-start.1 = ((bf16[128,3,2,6,128]{0,4,3,1,2:T(8,128)(2,1)}), bf16[128,3,2,6,128]{0,4,3,1,2:T(8,128)(2,1)S(1)}, u32[]{:S(2)}, u32[]{:S(2)}) async-start(bf16[128,3,2,6,128]{0,4,3,1,2:T(8,128)(2,1)} %copy.38), calls=%async_computation.1 | async-start | bytes 2359296 | tf_op jit(solution)/shard_map/all_to_all | solution.py:58
  14.7 0.8 copy.35
  15.4 0.8 all-to-all-done.1
  16.2 3.8 %all-to-all-start = ((bf16[32,2,2,6,128]{4,0,3,1,2:T(8,128)(2,1)}), bf16[32,2,2,6,128]{4,0,3,1,2:T(8,128)(2,1)S(1)}, u32[]{:S(2)}, u32[]{:S(2)}) async-start(bf16[32,2,2,6,128]{4,0,3,1,2:T(8,128)(2,1)} %copy.35), calls=%async_computation | async-start | bytes 393216 | tf_op jit(solution)/shard_map/all_to_all | solution.py:60
  20.8 1.7 %copy.43 = bf16[128,4608]{0,1:T(8,128)(2,1)S(1)} copy(bf16[128,4608]{1,0:T(8,128)(2,1)} %param.10) | data formatting | bytes 2359296 | tf_op args[1]
  22.5 1.1 %copy.44 = bf16[128,3,2,6,128]{0,4,3,1,2:T(8,128)(2,1)} copy(bf16[128,3,2,6,128]{0,4,3,2,1:T(8,128)(2,1)S(1)} %bitcast.91) | data formatting | bytes 2359296 | tf_op jit(solution)/shard_map/reshape | solution.py:53
  23.6 3.6 %all-to-all-start.3 = ((bf16[128,3,2,6,128]{0,4,3,1,2:T(8,128)(2,1)}), bf16[128,3,2,6,128]{0,4,3,1,2:T(8,128)(2,1)S(1)}, u32[]{:S(2)}, u32[]{:S(2)}) async-start(bf16[128,3,2,6,128]{0,4,3,1,2:T(8,128)(2,1)} %copy.44), calls=%async_computation.3 | async-start | bytes 2359296 | tf_op jit(solution)/shard_map/all_to_all | solution.py:59
  29.3 1.2 %reshape.36 = bf16[32,2,2,6,128]{4,3,2,1,0:T(8,128)(2,1)S(1)} reshape(bf16[32,3072]{1,0:T(8,128)(2,1)} %param.12) | data formatting | bytes 393216 | tf_op jit(solution)/shard_map/reshape | solution.py:55
  30.4 0.8 copy.46
  31.2 3.6 %all-to-all-start.4 = ((bf16[32,2,2,6,128]{4,0,3,1,2:T(8,128)(2,1)}), bf16[32,2,2,6,128]{4,0,3,1,2:T(8,128)(2,1)S(1)}, u32[]{:S(2)}, u32[]{:S(2)}) async-start(bf16[32,2,2,6,128]{4,0,3,1,2:T(8,128)(2,1)} %copy.46), calls=%async_computation.4 | async-start | bytes 393216 | tf_op jit(solution)/shard_map/all_to_all | solution.py:61
  34.8 1.4 %copy.45 = bf16[2,128,3,1,6,128]{5,1,0,4,2,3:T(8,128)(2,1)} copy(bf16[2,128,3,1,6,128]{1,5,4,2,0,3:T(8,128)(2,1)S(1)} %bitcast.88) | data formatting | bytes 2359296 | tf_op jit(solution)/shard_map/all_to_all | solution.py:59
  36.5 1.1 copy-done.1
  38.4 0.8 fusion.43
  40.9 1.1 %copy.48 = bf16[256,6,128]{2,1,0:T(8,128)(2,1)} copy(bf16[256,6,128]{0,2,1:T(8,128)(2,1)S(1)} %fusion.13) | data formatting | bytes 786432 | tf_op jit(solution)/shard_map/convert_element_type | solution.py:30
  42.0 3.5 %all-to-all-start.5 = ((bf16[256,6,128]{2,1,0:T(8,128)(2,1)}), bf16[256,6,128]{2,1,0:T(8,128)(2,1)S(1)}, u32[]{:S(2)}, u32[]{:S(2)}) async-start(bf16[256,6,128]{2,1,0:T(8,128)(2,1)} %copy.48), calls=%async_computation.5 | async-start | bytes 1048576 | tf_op jit(solution)/shard_map/all_to_all | solution.py:79
  45.5 2.0 %fusion.12 = bf16[256,6,128]{0,2,1:T(8,128)(2,1)S(1)} fusion(bf16[256,6,128]{2,0,1:T(8,128)(2,1)S(1)} %get-tuple-element.6, bf16[64,6,128]{2,0,1:T(8,128)(2,1)S(1)} %copy-done.5, f32[6,256,320]{1,2,0:T(8,128)} %copy-done.6, f32[6,256]{1,0:T(8,128)S(1)} %get-tuple-element.12), kind=kOutput, calls=%fused_computation.20 | convolution fusion | flops 127991808 | bytes 2856960 | tf_op jit(solution)/shard_map/hqk,khd->qhd/dot_general | solution.py:26
  47.5 1.1 %copy.40 = bf16[256,6,128]{2,1,0:T(8,128)(2,1)} copy(bf16[256,6,128]{0,2,1:T(8,128)(2,1)S(1)} %fusion.12) | data formatting | bytes 786432 | tf_op jit(solution)/shard_map/convert_element_type | solution.py:30
  48.6 3.5 %all-to-all-start.2 = ((bf16[256,6,128]{2,1,0:T(8,128)(2,1)}), bf16[256,6,128]{2,1,0:T(8,128)(2,1)S(1)}, u32[]{:S(2)}, u32[]{:S(2)}) async-start(bf16[256,6,128]{2,1,0:T(8,128)(2,1)} %copy.40), calls=%async_computation.2 | async-start | bytes 1048576 | tf_op jit(solution)/shard_map/all_to_all | solution.py:78
  52.4 1.0 all-to-all-done.2
  54.5 39.8 %all-gather.2.cloned.1.call-done = bf16[1536,3072]{0,1:T(8,128)(2,1)} async-done(((bf16[1536,192]{0,1:T(8,128)(2,1)}), bf16[1536,3072]{0,1:T(8,128)(2,1)}) %all-gather.2.cloned.1.call-update) | async-done | bytes 9437200 | tf_op jit(solution)/shard_map/all_gather | solution.py:86
  94.3 5.2 %fusion.20 = f32[256,3072]{1,0:T(8,128)S(1)} fusion(bf16[1536,3072]{0,1:T(8,128)(2,1)} %all-gather.2.cloned.1.call-done, bf16[128,1536]{0,1:T(8,128)(2,1)S(1)} %bitcast.103, bf16[128,1536]{0,1:T(8,128)(2,1)S(1)} %bitcast.104), kind=kOutput, calls=%fused_computation.28 | convolution fusion | flops 2417491968 | bytes 13369344 | tf_op jit(solution)/shard_map/dot_general | solution.py:34
  99.5 1.4 %fusion.9 = (bf16[128,3072]{1,0:T(8,128)(2,1)}, bf16[128,3072]{1,0:T(8,128)(2,1)}) fusion(f32[256,3072]{1,0:T(8,128)S(1)} %fusion.20, f32[3072]{0:T(1024)S(1)} %bitcast.105), kind=kLoop, calls=%fused_computation.14 | loop fusion | flops 1572864 | bytes 4730880 | tf_op jit(solution)/shard_map/convert_element_type | solution.py:89
  (38 shorter events, 5.9 us)
Async XLA Ops:
  7.2 47.3 %copy-start = (f32[64,3072]{1,0:T(8,128)S(1)}, f32[64,3072]{1,0:T(8,128)}, u32[]{:S(2)}) copy-start(f32[64,3072]{1,0:T(8,128)} %param.14) | copy-start | bytes 2359300
  7.2 87.1 %all-gather.2.cloned.1.call-start = ((), (), s32[]{:S(2)}) async-start(), calls=%async_computation.6 | async-start | bytes 10027008 | tf_op jit(solution)/shard_map/all_gather | solution.py:86
  9.6 4.8 %copy-start.3 = (bf16[32,3072]{1,0:T(8,128)(2,1)S(1)}, bf16[32,3072]{1,0:T(8,128)(2,1)}, u32[]{:S(2)}) copy-start(bf16[32,3072]{1,0:T(8,128)(2,1)} %param.11) | copy-start | bytes 589828
  10.8 5.5 %all-to-all-start.1 = ((bf16[128,3,2,6,128]{0,4,3,1,2:T(8,128)(2,1)}), bf16[128,3,2,6,128]{0,4,3,1,2:T(8,128)(2,1)S(1)}, u32[]{:S(2)}, u32[]{:S(2)}) async-start(bf16[128,3,2,6,128]{0,4,3,1,2:T(8,128)(2,1)} %copy.38), calls=%async_computation.1 | async-start | bytes 2359296 | tf_op jit(solution)/shard_map/all_to_all | solution.py:58
  16.2 7.4 %all-to-all-start = ((bf16[32,2,2,6,128]{4,0,3,1,2:T(8,128)(2,1)}), bf16[32,2,2,6,128]{4,0,3,1,2:T(8,128)(2,1)S(1)}, u32[]{:S(2)}, u32[]{:S(2)}) async-start(bf16[32,2,2,6,128]{4,0,3,1,2:T(8,128)(2,1)} %copy.35), calls=%async_computation | async-start | bytes 393216 | tf_op jit(solution)/shard_map/all_to_all | solution.py:60
  23.6 7.6 %all-to-all-start.3 = ((bf16[128,3,2,6,128]{0,4,3,1,2:T(8,128)(2,1)}), bf16[128,3,2,6,128]{0,4,3,1,2:T(8,128)(2,1)S(1)}, u32[]{:S(2)}, u32[]{:S(2)}) async-start(bf16[128,3,2,6,128]{0,4,3,1,2:T(8,128)(2,1)} %copy.44), calls=%async_computation.3 | async-start | bytes 2359296 | tf_op jit(solution)/shard_map/all_to_all | solution.py:59
  31.2 5.1 %copy-start.2 = (bf16[2,32,2,1,6,128]{5,1,0,4,2,3:T(8,128)(2,1)S(1)}, bf16[2,32,2,1,6,128]{5,1,0,4,2,3:T(8,128)(2,1)}, u32[]{:S(2)}) copy-start(bf16[2,32,2,1,6,128]{5,1,0,4,2,3:T(8,128)(2,1)} %copy.36) | copy-start | bytes 589828
  31.2 5.0 %all-to-all-start.4 = ((bf16[32,2,2,6,128]{4,0,3,1,2:T(8,128)(2,1)}), bf16[32,2,2,6,128]{4,0,3,1,2:T(8,128)(2,1)S(1)}, u32[]{:S(2)}, u32[]{:S(2)}) async-start(bf16[32,2,2,6,128]{4,0,3,1,2:T(8,128)(2,1)} %copy.46), calls=%async_computation.4 | async-start | bytes 393216 | tf_op jit(solution)/shard_map/all_to_all | solution.py:61
  36.2 1.3 %copy-start.1 = (bf16[2,128,3,1,6,128]{5,1,0,4,2,3:T(8,128)(2,1)S(1)}, bf16[2,128,3,1,6,128]{5,1,0,4,2,3:T(8,128)(2,1)}, u32[]{:S(2)}) copy-start(bf16[2,128,3,1,6,128]{5,1,0,4,2,3:T(8,128)(2,1)} %copy.45) | copy-start | bytes 3538948
  36.4 3.4 %copy-start.4 = (bf16[64,6,128]{2,0,1:T(8,128)(2,1)}, bf16[64,6,128]{2,0,1:T(8,128)(2,1)S(1)}, u32[]{:S(2)}) copy-start(bf16[64,6,128]{2,0,1:T(8,128)(2,1)S(1)} %get-tuple-element.10) | copy-start | bytes 294916
  39.2 1.3 %copy-start.6 = (f32[6,256,320]{1,2,0:T(8,128)}, f32[6,256,320]{1,2,0:T(8,128)S(1)}, u32[]{:S(2)}) copy-start(f32[6,256,320]{1,2,0:T(8,128)S(1)} %get-tuple-element.13) | copy-start | bytes 5898244
  40.9 4.6 %copy-start.5 = (bf16[64,6,128]{2,0,1:T(8,128)(2,1)S(1)}, bf16[64,6,128]{2,0,1:T(8,128)(2,1)}, u32[]{:S(2)}) copy-start(bf16[64,6,128]{2,0,1:T(8,128)(2,1)} %copy-done.4) | copy-start | bytes 294916
  42.0 6.6 %all-to-all-start.5 = ((bf16[256,6,128]{2,1,0:T(8,128)(2,1)}), bf16[256,6,128]{2,1,0:T(8,128)(2,1)S(1)}, u32[]{:S(2)}, u32[]{:S(2)}) async-start(bf16[256,6,128]{2,1,0:T(8,128)(2,1)} %copy.48), calls=%async_computation.5 | async-start | bytes 1048576 | tf_op jit(solution)/shard_map/all_to_all | solution.py:79
  48.6 4.9 %all-to-all-start.2 = ((bf16[256,6,128]{2,1,0:T(8,128)(2,1)}), bf16[256,6,128]{2,1,0:T(8,128)(2,1)S(1)}, u32[]{:S(2)}, u32[]{:S(2)}) async-start(bf16[256,6,128]{2,1,0:T(8,128)(2,1)} %copy.40), calls=%async_computation.2 | async-start | bytes 1048576 | tf_op jit(solution)/shard_map/all_to_all | solution.py:78
Sparse Core Ops, SparseCore 0:
  10.3 83.9 all-gather.1
where the time goes:
time: 109 us; the launch traced here: 108 us
  waiting for transfers between devices  42.3 us (39%)
  starting transfers between devices  21.7 us (20%)
  between operations  16.2 us (15%)
  local copies, waits for them, and re-layouts  15.7 us (14%)
  matrix products  9.57 us (9%)
  other arithmetic  2.31 us (2%)
    all_gather x1, waiting for transfers between devices, body(): lax.all_gather(out_weight, ('blk', 'seq'), axis=1, tiled=True)  39.8 us
    dot_general x1, matrix products, column_projector(): jnp.dot(stacked_rows, shard_piece, preferred_element_type=jnp.float32)  5.25 us
    unnamed x16, local copies, waits for them, and re-layouts  4.64 us
    all_to_all x1, starting transfers between devices, body(): lax.all_to_all(text_primal, 'seq', split_axis=2, concat_axis=0, tiled=True)  3.79 us
    all_to_all x1, starting transfers between devices, body(): lax.all_to_all(image_primal, 'seq', split_axis=2, concat_axis=0, tiled=True)  3.65 us
    all_to_all x1, starting transfers between devices, body(): lax.all_to_all(image_tangent, 'seq', split_axis=2, concat_axis=0, tiled=T...  3.63 us
    all_to_all x1, starting transfers between devices, body(): lax.all_to_all(text_tangent, 'seq', split_axis=2, concat_axis=0, tiled=True)  3.58 us
    all_to_all x1, starting transfers between devices, body(): lax.all_to_all(attended, 'seq', split_axis=0, concat_axis=1, tiled=True)  3.5 us
  transfers between devices with their start and end apart: 7, of which 3 were waited for; matrix products, arithmetic and copies ran while one was open for 18% of the time, Pallas kernels for 0%

commit v1 on v0

--- a/solution.py
+++ b/solution.py
@@ -1,6 +1,8 @@
 import jax
 import jax.numpy as jnp
 from jax import lax
+from jax.experimental import pallas as pl
+from jax.experimental.pallas import tpu as pltpu
 from jax.sharding import PartitionSpec as P
 
 HS = 128
@@ -90,6 +92,382 @@
     return (output, output_tangent)
 
 
+MESH = pl.DeviceIdType.MESH
+DEPTH = 4
+QUARTERS = 4
+LAST = 13
+UP, DOWN, ACROSS, SIDE, CORE = 0, 1, 2, 3, 4
+
+
+def fused_kernel(
+    lengths,
+    shard,
+    image_qkv,
+    image_tan,
+    text_kv,
+    text_tan,
+    gate,
+    out,
+    out_tan,
+    weights,
+    queries,
+    keyvals,
+    attended,
+    send_sem,
+    recv_sem,
+    core_sem,
+    pair_send,
+    pair_recv,
+    local_sem,
+):
+    side = lax.axis_index("grp")
+    blk = lax.axis_index("blk")
+    core = lax.axis_index("seq")
+    plane, across = blk // 2, blk % 2
+    mate = 1 - core
+    width = HEADS * HS
+    rows = image_qkv.shape[0]
+    texts = text_kv.shape[0]
+    own_text, own_image = 2 * texts, 2 * texts + rows
+
+    def target(way):
+        if way == UP:
+            return (side, blk + 2, core)
+        if way == DOWN:
+            return (side, blk - 2, core)
+        if way == ACROSS:
+            return (side, plane * 2 + (1 - across), core)
+        if way == SIDE:
+            return (1 - side, blk, core)
+        return (side, blk, mate)
+
+    locals_ = [pltpu.make_async_copy(shard, weights.at[blk, core], local_sem.at[0])]
+    for part, (image, text) in enumerate(((image_qkv, text_kv), (image_tan, text_tan))):
+        locals_.append(
+            pltpu.make_async_copy(
+                image.at[:, pl.ds(0, width)], queries.at[part], local_sem.at[1 + 3 * part]
+            )
+        )
+        locals_.append(
+            pltpu.make_async_copy(
+                text, keyvals.at[part, pl.ds(0, texts)], local_sem.at[2 + 3 * part]
+            )
+        )
+        locals_.append(
+            pltpu.make_async_copy(
+                image.at[:, pl.ds(width, 2 * width)],
+                keyvals.at[part, pl.ds(own_text, rows)],
+                local_sem.at[3 + 3 * part],
+            )
+        )
+    for copy in locals_:
+        copy.start()
+
+    barrier = pltpu.get_barrier_semaphore()
+    for way in (ACROSS, SIDE, CORE):
+        pl.semaphore_signal(barrier, inc=1, device_id=target(way), device_id_type=MESH)
+
+    @pl.when(plane < DEPTH - 1)
+    def _():
+        pl.semaphore_signal(barrier, inc=1, device_id=target(UP), device_id_type=MESH)
+
+    @pl.when(plane > 0)
+    def _():
+        pl.semaphore_signal(barrier, inc=1, device_id=target(DOWN), device_id_type=MESH)
+
+    ends = (plane == 0).astype(jnp.int32) + (plane == DEPTH - 1).astype(jnp.int32)
+    pl.semaphore_wait(barrier, 5 - ends)
+    locals_[0].wait()
+
+    def send(block, piece, way):
+        place = weights.at[block, core, piece]
+        arrived = core_sem if way == CORE else recv_sem
+        return pltpu.make_async_remote_copy(
+            src_ref=place,
+            dst_ref=place,
+            send_sem=send_sem.at[block, piece, way],
+            recv_sem=arrived.at[block, piece],
+            device_id=target(way),
+            device_id_type=MESH,
+        )
+
+    def arrival(block, piece):
+        send(block, piece, ACROSS).wait_recv()
+
+    def mate_arrival(block, piece):
+        place = weights.at[block, mate, piece]
+        pltpu.make_async_remote_copy(
+            src_ref=place,
+            dst_ref=place,
+            send_sem=send_sem.at[block, piece, CORE],
+            recv_sem=core_sem.at[block, piece],
+            device_id=target(CORE),
+            device_id_type=MESH,
+        ).wait_recv()
+
+    def quarter(k):
+        return (k + 2 * side) % QUARTERS
+
+    other = plane * 2 + (1 - across)
+
+    def block_at(at, flip):
+        return at * 2 + (across + flip) % 2
+
+    def both_lines(block, piece, act):
+        @pl.when(plane < DEPTH - 1)
+        def _():
+            act(send(block, piece, UP))
+
+        @pl.when(plane > 0)
+        def _():
+            act(send(block, piece, DOWN))
+
+    def own_sends(act):
+        for k in range(QUARTERS):
+            piece = quarter(k)
+            if k < 2:
+                both_lines(blk, piece, act)
+            act(send(blk, piece, ACROSS))
+        for k in range(QUARTERS):
+            act(send(blk, quarter(k), CORE))
+
+    def stage(j, wait, act):
+        @pl.when(j < QUARTERS)
+        def _():
+            piece = quarter(j)
+            wait(other, piece)
+
+            @pl.when(j == 0)
+            def _():
+                both_lines(other, piece, act)
+
+            act(send(other, piece, CORE))
+
+        @pl.when(j < 3 * (DEPTH - 1))
+        def _():
+            step, item = j // 3 + 1, j % 3
+            flip, piece = item // 2, quarter(item % 2)
+            for way, at in ((UP, plane - step), (DOWN, plane + step)):
+
+                @pl.when((at >= 0) & (at < DEPTH))
+                def _():
+                    block = block_at(at, flip)
+                    wait(block, piece)
+                    more = plane < DEPTH - 1 if way == UP else plane > 0
+
+                    @pl.when(more)
+                    def _():
+                        act(send(block, piece, way))
+
+                    act(send(block, piece, SIDE))
+
+                    @pl.when(item == 1)
+                    def _():
+                        act(send(block, piece, ACROSS))
+
+                    act(send(block, piece, CORE))
+
+        late = j - 2
+
+        @pl.when((late >= 0) & (late < 3 * (DEPTH - 1)))
+        def _():
+            step, item = (j + 1) // 3, (j + 1) % 3
+            flip, piece = item // 2, quarter(item % 2 + 2)
+            for at in (plane - step, plane + step):
+
+                @pl.when((at >= 0) & (at < DEPTH))
+                def _():
+                    block = block_at(at, flip)
+                    wait(block, piece)
+
+                    @pl.when(item == 1)
+                    def _():
+                        act(send(block, piece, ACROSS))
+
+                    act(send(block, piece, CORE))
+
+        @pl.when((j >= 4) & (j < 4 + 3 * (DEPTH - 1)) & ((j + 2) % 3 == 1))
+        def _():
+            step = (j + 2) // 3 - 1
+            for at in (plane - step, plane + step):
+
+                @pl.when((at >= 0) & (at < DEPTH))
+                def _():
+                    block = block_at(at, 1)
+                    for k in (1, 3):
+                        piece = quarter(k)
+                        wait(block, piece)
+                        act(send(block, piece, CORE))
+
+    pair = []
+    for part, (image, text) in enumerate(((image_qkv, text_kv), (image_tan, text_tan))):
+        for nth, (source, place) in enumerate(
+            (
+                (text, keyvals.at[part, pl.ds(texts, texts)]),
+                (image.at[:, pl.ds(width, 2 * width)], keyvals.at[part, pl.ds(own_image, rows)]),
+            )
+        ):
+            pair.append(
+                pltpu.make_async_remote_copy(
+                    src_ref=source,
+                    dst_ref=place,
+                    send_sem=pair_send.at[2 * part + nth],
+                    recv_sem=pair_recv.at[2 * part + nth],
+                    device_id=target(CORE),
+                    device_id_type=MESH,
+                )
+            )
+    for copy in pair:
+        copy.start()
+    own_sends(lambda copy: copy.start())
+    for copy in locals_[1:]:
+        copy.wait()
+    for copy in pair:
+        copy.wait()
+
+    image_live, text_live = lengths[0], lengths[1]
+    count = 2 * (texts + rows)
+    slot = lax.broadcasted_iota(jnp.int32, (1, count), 1)
+    text_at = slot + jnp.where(slot < texts, core * texts, mate * texts - texts)
+    image_at = slot - own_text + jnp.where(slot < own_image, core * rows, mate * rows - rows)
+    position = jnp.where(slot < own_text, text_at, image_at)
+    room = jnp.where(slot < own_text, text_live, image_live) - position
+
+    def one_head(head):
+        factor = HS ** (-0.5)
+        lanes = pl.ds(pl.multiple_of(head * HS, HS), HS)
+        value_lanes = pl.ds(pl.multiple_of(width + head * HS, HS), HS)
+        q, dq = queries[0, :, lanes], queries[1, :, lanes]
+        k, dk = keyvals[0, :, lanes], keyvals[1, :, lanes]
+        v, dv = keyvals[0, :, value_lanes], keyvals[1, :, value_lanes]
+        nt = (((1,), (1,)), ((), ()))
+        scores = lax.dot_general(q, k, nt, preferred_element_type=jnp.float32) * factor
+        tangent = (
+            lax.dot_general(
+                jnp.concatenate([dq, q], axis=1),
+                jnp.concatenate([k, dk], axis=1),
+                nt,
+                preferred_element_type=jnp.float32,
+            )
+            * factor
+        )
+        usable = jnp.broadcast_to(room, scores.shape) > 0
+        masked = jnp.where(usable, scores, -1e30)
+        highest = jnp.max(masked, axis=-1, keepdims=True)
+        raised = jnp.where(usable, jnp.exp(masked - highest), 0.0)
+        weight = raised * (1.0 / jnp.sum(raised, axis=-1, keepdims=True))
+        probs = weight.astype(jnp.bfloat16)
+        product = weight * tangent
+        mean = jnp.sum(product, axis=-1, keepdims=True)
+        tangent_probs = (product - weight * mean).astype(jnp.bfloat16)
+        both = jnp.dot(
+            probs, jnp.concatenate([v, dv], axis=1), preferred_element_type=jnp.float32
+        )
+        moved = jnp.dot(tangent_probs, v, preferred_element_type=jnp.float32)
+        attended[pl.ds(0, rows), lanes] = both[:, :HS].astype(jnp.bfloat16)
+        attended[pl.ds(rows, rows), lanes] = (moved + both[:, HS:]).astype(jnp.bfloat16)
+
+    def project(block):
+        for k in range(QUARTERS):
+            mate_arrival(block, k)
+        share = weights[block]
+        size = 2 * shard.shape[0] * shard.shape[1]
+        columns = pl.ds(pl.multiple_of(block * size, 128), size)
+        made = lax.dot_general(
+            attended[...],
+            share.reshape(size, width),
+            (((1,), (1,)), ((), ())),
+            preferred_element_type=jnp.float32,
+        )
+        made = (made * gate[:, columns]).astype(jnp.bfloat16)
+        out[:, columns] = made[:rows]
+        out_tan[:, columns] = made[rows:]
+
+    def loop(j, carry):
+        stage(j, arrival, lambda copy: copy.start())
+
+        @pl.when(j < HEADS // 2)
+        def _():
+            one_head(2 * j)
+            one_head(2 * j + 1)
+
+        @pl.when(j >= HEADS // 2)
+        def _():
+            nth = j - HEADS // 2
+            at = plane + (1 - 2 * (nth % 2)) * ((nth + 1) // 2)
+
+            @pl.when((at >= 0) & (at < DEPTH))
+            def _():
+                def one(flip, carry):
+                    project(block_at(at, flip))
+                    return carry
+
+                lax.fori_loop(0, 2, one, 0)
+
+        return carry
+
+    lax.fori_loop(0, LAST, loop, 0)
+
+    own_sends(lambda copy: copy.wait_send())
+
+    def drain(j, carry):
+        stage(j, lambda block, piece: None, lambda copy: copy.wait_send())
+        return carry
+
+    lax.fori_loop(0, LAST, drain, 0)
+
+
+def fused_body(
+    image_qkv,
+    image_qkv_tangent,
+    text_kv,
+    text_kv_tangent,
+    out_weight,
+    gate_table,
+    timesteps,
+    image_lengths,
+    text_lengths,
+):
+    rows, texts = image_qkv.shape[0], text_kv.shape[0]
+    width, share = out_weight.shape
+    blocks = lax.axis_size("blk")
+    features = gate_table.shape[1]
+    shard = out_weight.T.reshape(QUARTERS, share // QUARTERS, width)
+    gate_row = lax.dynamic_index_in_dim(gate_table, timesteps[0], 0, keepdims=True)
+    lengths = jnp.concatenate([image_lengths, text_lengths])
+    whole = pl.BlockSpec(memory_space=pl.ANY)
+    vmem = pl.BlockSpec(memory_space=pltpu.VMEM)
+    made = jax.ShapeDtypeStruct((rows, features), jnp.bfloat16)
+    return tuple(
+        pl.pallas_call(
+            fused_kernel,
+            out_shape=(made, made),
+            in_specs=[pl.BlockSpec(memory_space=pltpu.SMEM)] + [whole] * 5 + [vmem],
+            out_specs=(vmem, vmem),
+            scratch_shapes=[
+                pltpu.VMEM((blocks, 2, QUARTERS, share // QUARTERS, width), jnp.bfloat16),
+                pltpu.VMEM((2, rows, width), jnp.bfloat16),
+                pltpu.VMEM((2, 2 * (rows + texts), 2 * width), jnp.bfloat16),
+                pltpu.VMEM((2 * rows, width), jnp.bfloat16),
+                pltpu.SemaphoreType.DMA((blocks, QUARTERS, 5)),
+                pltpu.SemaphoreType.DMA((blocks, QUARTERS)),
+                pltpu.SemaphoreType.DMA((blocks, QUARTERS)),
+                pltpu.SemaphoreType.DMA((4,)),
+                pltpu.SemaphoreType.DMA((4,)),
+                pltpu.SemaphoreType.DMA((7,)),
+            ],
+            compiler_params=pltpu.CompilerParams(
+                collective_id=0, has_side_effects=True, vmem_limit_bytes=44 * 1024 * 1024
+            ),
+        )(lengths, shard, image_qkv, image_qkv_tangent, text_kv, text_kv_tangent, gate_row)
+    )
+
+
+def fits(mesh):
+    sizes = dict(mesh.shape)
+    return sizes["grp"] == 2 and sizes["seq"] == 2 and sizes["blk"] == 2 * DEPTH
+
+
 def solution(mesh):
     in_specs = (
         P(("grp", "blk", "seq"), None),
@@ -103,4 +481,5 @@
         P(("grp", "blk")),
     )
     out_specs = (P(("grp", "blk", "seq"), None), P(("grp", "blk", "seq"), None))
-    return jax.shard_map(body, mesh=mesh, in_specs=in_specs, out_specs=out_specs, check_vma=False)
+    chosen = fused_body if fits(mesh) else body
+    return jax.shard_map(chosen, mesh=mesh, in_specs=in_specs, out_specs=out_specs, check_vma=False)

time: 109 us -> 59.1 us (0.54)
  Pallas kernels: 0 us -> 48.8 us
  waiting for transfers between devices: 42.3 us -> 0 us
  starting transfers between devices: 21.7 us -> 0 us
  between operations: 16.2 us -> 2.68 us
  matrix products: 9.57 us -> 0 us
  local copies, waits for them, and re-layouts: 15.7 us -> 7.24 us
  other arithmetic: 2.31 us -> 0.08 us
    pallas_call x0 -> x1, Pallas kernels: none -> 48.8 us  [fused_body(): pl.pallas_call(fused_kernel, out_shape=(made, made), in_specs=[pl.BlockSp...]
    all_gather x1 -> x0, waiting for transfers between devices: 39.8 us -> none  [body(): lax.all_gather(out_weight, ('blk', 'seq'), axis=1, tiled=True)]
    all_to_all x6 -> x0, starting transfers between devices: 21.7 us -> none  [the longest x1 3.79 us: body(): lax.all_to_all(text_primal, 'seq', split_axis=2, concat_axis=0, tiled=True)]
    dot_general x7 -> x0, matrix products: 9.57 us -> none  [the longest x1 5.25 us: column_projector(): jnp.dot(stacked_rows, shard_piece, preferred_element_type=jnp.float32)]
    reshape x6 -> x0, local copies, waits for them, and re-layouts: 5.21 us -> none  [the longest x2 1.94 us: body(): text_kv_tangent.reshape(text_count, 2, seq_count, local_heads, HS)]
    all_to_all x6 -> x0, local copies, waits for them, and re-layouts: 3.53 us -> none  [the longest x1 1.44 us: body(): lax.all_to_all(image_tangent, 'seq', split_axis=2, concat_axis=0, tiled=T...]
    unnamed x16 -> x14, local copies, waits for them, and re-layouts: 4.64 us -> 7.22 us
    convert_element_type x2 -> x0, local copies, waits for them, and re-layouts: 2.17 us -> none  [the longest x1 1.09 us: attend(): tangent_attended.astype(jnp.bfloat16)]
  transfers between devices with their start and end apart: 7 -> 0, of which waited for: 3 -> 0; matrix products, arithmetic and copies ran while one was open for 18% -> 0% of each run, Pallas kernels for 0% -> 0%
where the time goes in v1:
time: 59.1 us; the launch traced here: 58.8 us
  Pallas kernels  48.8 us (83%)
  local copies, waits for them, and re-layouts  7.24 us (12%)
  between operations  2.68 us (5%)
    pallas_call x1, Pallas kernels, fused_body(): pl.pallas_call(fused_kernel, out_shape=(made, made), in_specs=[pl.BlockSp...  48.8 us
    unnamed x14, local copies, waits for them, and re-layouts  7.22 us

profile of v1, /device:TPU:1, one launch (start us, length us, event | category | flops | bytes accessed | tf_op | source)
XLA Modules:
  0.0 58.8 jit_solution(15650689722311285458)
XLA Ops:
  0.6 0.0 copy-start
  2.7 0.1 pad_add_fusion.lengths
  2.7 0.0 copy-done
  2.8 0.0 copy-start.1
  2.8 1.3 %copy-done.1 = bf16[128,4608]{1,0:T(8,128)(2,1)S(1)} copy-done((bf16[128,4608]{1,0:T(8,128)(2,1)S(1)}, bf16[128,4608]{1,0:T(8,128)(2,1)}, u32[]{:S(2)}) %copy-start.1) | copy-done | bytes 1179672
  4.0 0.0 copy-start.2
  4.0 1.3 %copy-done.2 = bf16[128,4608]{1,0:T(8,128)(2,1)S(1)} copy-done((bf16[128,4608]{1,0:T(8,128)(2,1)S(1)}, bf16[128,4608]{1,0:T(8,128)(2,1)}, u32[]{:S(2)}) %copy-start.2) | copy-done | bytes 1179672
  5.3 0.0 copy-start.3
  5.3 1.1 %copy-done.3 = bf16[1536,192]{0,1:T(8,128)(2,1)S(1)} copy-done((bf16[1536,192]{0,1:T(8,128)(2,1)S(1)}, bf16[1536,192]{0,1:T(8,128)(2,1)}, u32[]{:S(2)}) %copy-start.3) | copy-done | bytes 589848
  6.4 0.0 copy-start.4
  6.4 0.9 %copy-done.4 = bf16[32,3072]{1,0:T(8,128)(2,1)S(1)} copy-done((bf16[32,3072]{1,0:T(8,128)(2,1)S(1)}, bf16[32,3072]{1,0:T(8,128)(2,1)}, u32[]{:S(2)}) %copy-start.4) | copy-done | bytes 196632
  7.3 0.0 copy-start.5
  7.3 0.9 %copy-done.5 = bf16[32,3072]{1,0:T(8,128)(2,1)S(1)} copy-done((bf16[32,3072]{1,0:T(8,128)(2,1)S(1)}, bf16[32,3072]{1,0:T(8,128)(2,1)}, u32[]{:S(2)}) %copy-start.5) | copy-done | bytes 196632
  8.2 48.8 %shard_map.104 = (bf16[128,3072]{1,0:T(8,128)(2,1)S(1)}, bf16[128,3072]{1,0:T(8,128)(2,1)S(1)}) custom-call(s32[2]{0:T(128)S(1)} %pad_add_fusion.lengths, bf16[4,48,1536]{2,1,0:T(8,128)(2,1)S(1)} %bitcast.7, bf16[128,4608]{1,0:T(8,128)(2,1)S(1)} %copy-done.1, bf16[128,4608]{1,0:T(8,128)(2,1)S(1)} %copy-done.2, bf16[32,3072]{1,0:T(8,128)(2,1)S(1)} %copy-done.4, ...), custom_call_target="tpu_custom_call" | custom-call | tf_op jit(solution)/shard_map/pallas_call | solution.py:442
  57.0 0.9 %copy.16 = bf16[128,3072]{1,0:T(8,128)(2,1)} copy(bf16[128,3072]{1,0:T(8,128)(2,1)S(1)} %get-tuple-element.4) | data formatting | bytes 1572864
  57.9 0.9 %copy.17 = bf16[128,3072]{1,0:T(8,128)(2,1)} copy(bf16[128,3072]{1,0:T(8,128)(2,1)S(1)} %get-tuple-element.5) | data formatting | bytes 1572864
  (1 shorter events, 0.0 us)
Async XLA Ops:
  0.6 2.1 %copy-start = (f32[64,3072]{1,0:T(8,128)S(1)}, f32[64,3072]{1,0:T(8,128)}, u32[]{:S(2)}) copy-start(f32[64,3072]{1,0:T(8,128)} %param.14) | copy-start | bytes 2359300
  2.8 1.3 %copy-start.1 = (bf16[128,4608]{1,0:T(8,128)(2,1)S(1)}, bf16[128,4608]{1,0:T(8,128)(2,1)}, u32[]{:S(2)}) copy-start(bf16[128,4608]{1,0:T(8,128)(2,1)} %image_qkv.1) | copy-start | bytes 3538948
  4.0 1.3 %copy-start.2 = (bf16[128,4608]{1,0:T(8,128)(2,1)S(1)}, bf16[128,4608]{1,0:T(8,128)(2,1)}, u32[]{:S(2)}) copy-start(bf16[128,4608]{1,0:T(8,128)(2,1)} %image_tan.1) | copy-start | bytes 3538948
  5.3 1.1 %copy-start.3 = (bf16[1536,192]{0,1:T(8,128)(2,1)S(1)}, bf16[1536,192]{0,1:T(8,128)(2,1)}, u32[]{:S(2)}) copy-start(bf16[1536,192]{0,1:T(8,128)(2,1)} %param.13) | copy-start | bytes 1769476
  6.4 0.9 %copy-start.4 = (bf16[32,3072]{1,0:T(8,128)(2,1)S(1)}, bf16[32,3072]{1,0:T(8,128)(2,1)}, u32[]{:S(2)}) copy-start(bf16[32,3072]{1,0:T(8,128)(2,1)} %text_kv.1) | copy-start | bytes 589828
  7.3 0.9 %copy-start.5 = (bf16[32,3072]{1,0:T(8,128)(2,1)S(1)}, bf16[32,3072]{1,0:T(8,128)(2,1)}, u32[]{:S(2)}) copy-start(bf16[32,3072]{1,0:T(8,128)(2,1)} %text_tan.1) | copy-start | bytes 589828

commit v2 on v1

--- a/solution.py
+++ b/solution.py
@@ -96,23 +96,27 @@
 DEPTH = 4
 QUARTERS = 4
 LAST = 13
+LAG = 4
 UP, DOWN, ACROSS, SIDE, CORE = 0, 1, 2, 3, 4
 
 
 def fused_kernel(
-    lengths,
+    timesteps,
+    image_lengths,
+    text_lengths,
     shard,
     image_qkv,
     image_tan,
     text_kv,
     text_tan,
-    gate,
+    gate_table,
     out,
     out_tan,
     weights,
     queries,
     keyvals,
     attended,
+    gate,
     send_sem,
     recv_sem,
     core_sem,
@@ -160,6 +164,7 @@
                 local_sem.at[3 + 3 * part],
             )
         )
+    locals_.append(pltpu.make_async_copy(gate_table, gate, local_sem.at[7]))
     for copy in locals_:
         copy.start()
 
@@ -228,6 +233,8 @@
             if k < 2:
                 both_lines(blk, piece, act)
             act(send(blk, piece, ACROSS))
+
+    def own_to_mate(act):
         for k in range(QUARTERS):
             act(send(blk, quarter(k), CORE))
 
@@ -317,15 +324,13 @@
                     device_id_type=MESH,
                 )
             )
+    own_sends(lambda copy: copy.start())
     for copy in pair:
         copy.start()
-    own_sends(lambda copy: copy.start())
-    for copy in locals_[1:]:
-        copy.wait()
-    for copy in pair:
-        copy.wait()
-
-    image_live, text_live = lengths[0], lengths[1]
+    own_to_mate(lambda copy: copy.start())
+
+    image_live, text_live = image_lengths[0], text_lengths[0]
+    level = timesteps[0]
     count = 2 * (texts + rows)
     slot = lax.broadcasted_iota(jnp.int32, (1, count), 1)
     text_at = slot + jnp.where(slot < texts, core * texts, mate * texts - texts)
@@ -379,12 +384,23 @@
             (((1,), (1,)), ((), ())),
             preferred_element_type=jnp.float32,
         )
-        made = (made * gate[:, columns]).astype(jnp.bfloat16)
+        made = (made * gate[pl.ds(level, 1), columns]).astype(jnp.bfloat16)
         out[:, columns] = made[:rows]
         out_tan[:, columns] = made[rows:]
 
+    def drain(j, carry):
+        stage(j, lambda block, piece: None, lambda copy: copy.wait_send())
+        return carry
+
     def loop(j, carry):
         stage(j, arrival, lambda copy: copy.start())
+
+        @pl.when(j == 0)
+        def _():
+            for copy in locals_[1:]:
+                copy.wait()
+            for copy in pair:
+                copy.wait()
 
         @pl.when(j < HEADS // 2)
         def _():
@@ -404,17 +420,18 @@
 
                 lax.fori_loop(0, 2, one, 0)
 
+        @pl.when(j >= LAG)
+        def _():
+            drain(j - LAG, 0)
+
         return carry
 
     lax.fori_loop(0, LAST, loop, 0)
 
     own_sends(lambda copy: copy.wait_send())
-
-    def drain(j, carry):
-        stage(j, lambda block, piece: None, lambda copy: copy.wait_send())
-        return carry
-
-    lax.fori_loop(0, LAST, drain, 0)
+    own_to_mate(lambda copy: copy.wait_send())
+
+    lax.fori_loop(LAST - LAG, LAST, drain, 0)
 
 
 def fused_body(
@@ -433,8 +450,6 @@
     blocks = lax.axis_size("blk")
     features = gate_table.shape[1]
     shard = out_weight.T.reshape(QUARTERS, share // QUARTERS, width)
-    gate_row = lax.dynamic_index_in_dim(gate_table, timesteps[0], 0, keepdims=True)
-    lengths = jnp.concatenate([image_lengths, text_lengths])
     whole = pl.BlockSpec(memory_space=pl.ANY)
     vmem = pl.BlockSpec(memory_space=pltpu.VMEM)
     made = jax.ShapeDtypeStruct((rows, features), jnp.bfloat16)
@@ -442,24 +457,35 @@
         pl.pallas_call(
             fused_kernel,
             out_shape=(made, made),
-            in_specs=[pl.BlockSpec(memory_space=pltpu.SMEM)] + [whole] * 5 + [vmem],
+            in_specs=[pl.BlockSpec(memory_space=pltpu.SMEM)] * 3 + [whole] * 6,
             out_specs=(vmem, vmem),
             scratch_shapes=[
                 pltpu.VMEM((blocks, 2, QUARTERS, share // QUARTERS, width), jnp.bfloat16),
                 pltpu.VMEM((2, rows, width), jnp.bfloat16),
                 pltpu.VMEM((2, 2 * (rows + texts), 2 * width), jnp.bfloat16),
                 pltpu.VMEM((2 * rows, width), jnp.bfloat16),
+                pltpu.VMEM(gate_table.shape, jnp.float32),
                 pltpu.SemaphoreType.DMA((blocks, QUARTERS, 5)),
                 pltpu.SemaphoreType.DMA((blocks, QUARTERS)),
                 pltpu.SemaphoreType.DMA((blocks, QUARTERS)),
                 pltpu.SemaphoreType.DMA((4,)),
                 pltpu.SemaphoreType.DMA((4,)),
-                pltpu.SemaphoreType.DMA((7,)),
+                pltpu.SemaphoreType.DMA((8,)),
             ],
             compiler_params=pltpu.CompilerParams(
-                collective_id=0, has_side_effects=True, vmem_limit_bytes=44 * 1024 * 1024
+                collective_id=0, has_side_effects=True, vmem_limit_bytes=60 * 1024 * 1024
             ),
-        )(lengths, shard, image_qkv, image_qkv_tangent, text_kv, text_kv_tangent, gate_row)
+        )(
+            timesteps,
+            image_lengths,
+            text_lengths,
+            shard,
+            image_qkv,
+            image_qkv_tangent,
+            text_kv,
+            text_kv_tangent,
+            gate_table,
+        )
     )
 
 

time: 59.1 us -> 53.7 us (0.909)
  local copies, waits for them, and re-layouts: 7.24 us -> 3.02 us
  Pallas kernels: 48.8 us -> 48 us
    unnamed x14 -> x4, local copies, waits for them, and re-layouts: 7.22 us -> 3.02 us
    pallas_call x1, Pallas kernels: 48.8 us -> 48 us  [fused_body(): pl.pallas_call(fused_kernel, out_shape=(made, made), in_specs=[pl.BlockSp...]
where the time goes in v2:
time: 53.7 us; the launch traced here: 53.6 us
  Pallas kernels  48 us (89%)
  local copies, waits for them, and re-layouts  3.02 us (6%)
  between operations  2.59 us (5%)
    pallas_call x1, Pallas kernels, fused_body(): pl.pallas_call(fused_kernel, out_shape=(made, made), in_specs=[pl.BlockSp...  48 us
    unnamed x4, local copies, waits for them, and re-layouts  3.02 us

profile of v2, /device:TPU:1, one launch (start us, length us, event | category | flops | bytes accessed | tf_op | source)
XLA Modules:
  0.0 53.6 jit_solution(15610474459987985286)
XLA Ops:
  2.6 48.0 %shard_map.104 = (bf16[128,3072]{1,0:T(8,128)(2,1)}, bf16[128,3072]{1,0:T(8,128)(2,1)}) custom-call(s32[1]{0:T(128)S(6)} %copy.13.timesteps, s32[1]{0:T(128)S(6)} %copy.14.image_lengths, s32[1]{0:T(128)S(6)} %copy.15.text_lengths, bf16[4,48,1536]{2,1,0:T(8,128)(2,1)} %bitcast.3, bf16[128,4608]{1,0:T(8,128)(2,1)} %image_qkv.1, bf16[128,4608]{1,0:T(8,128)(2,1)} %image_tan.1, ...), custom_call_target="tpu_custom_call" | custom-call | tf_op jit(solution)/shard_map/pallas_call | solution.py:457
  50.5 0.0 copy-start
  50.5 2.1 %copy.16 = bf16[128,3072]{1,0:T(8,128)(2,1)} copy(bf16[128,3072]{1,0:T(8,128)(2,1)} %get-tuple-element.4) | data formatting | bytes 1572864
  52.7 0.0 copy-done
  52.7 0.9 %copy.17 = bf16[128,3072]{1,0:T(8,128)(2,1)} copy(bf16[128,3072]{1,0:T(8,128)(2,1)S(1)} %copy-done) | data formatting | bytes 1572864
Async XLA Ops:
  50.5 2.1 %copy-start = (bf16[128,3072]{1,0:T(8,128)(2,1)S(1)}, bf16[128,3072]{1,0:T(8,128)(2,1)}, u32[]{:S(2)}) copy-start(bf16[128,3072]{1,0:T(8,128)(2,1)} %get-tuple-element.5) | copy-start | bytes 2359300

commit v3 on v2

--- a/solution.py
+++ b/solution.py
@@ -117,6 +117,8 @@
     keyvals,
     attended,
     gate,
+    held,
+    out_sem,
     send_sem,
     recv_sem,
     core_sem,
@@ -372,6 +374,18 @@
         attended[pl.ds(0, rows), lanes] = both[:, :HS].astype(jnp.bfloat16)
         attended[pl.ds(rows, rows), lanes] = (moved + both[:, HS:]).astype(jnp.bfloat16)
 
+    def leave(block):
+        size = 2 * shard.shape[0] * shard.shape[1]
+        columns = pl.ds(pl.multiple_of(block * size, 128), size)
+        return [
+            pltpu.make_async_copy(
+                held.at[pl.ds(part * rows, rows), columns],
+                place.at[:, columns],
+                out_sem.at[block, part],
+            )
+            for part, place in enumerate((out, out_tan))
+        ]
+
     def project(block):
         for k in range(QUARTERS):
             mate_arrival(block, k)
@@ -385,8 +399,9 @@
             preferred_element_type=jnp.float32,
         )
         made = (made * gate[pl.ds(level, 1), columns]).astype(jnp.bfloat16)
-        out[:, columns] = made[:rows]
-        out_tan[:, columns] = made[rows:]
+        held[:, columns] = made
+        for copy in leave(block):
+            copy.start()
 
     def drain(j, carry):
         stage(j, lambda block, piece: None, lambda copy: copy.wait_send())
@@ -432,6 +447,13 @@
     own_to_mate(lambda copy: copy.wait_send())
 
     lax.fori_loop(LAST - LAG, LAST, drain, 0)
+
+    def left(block, carry):
+        for copy in leave(block):
+            copy.wait()
+        return carry
+
+    lax.fori_loop(0, 2 * DEPTH, left, 0)
 
 
 def fused_body(
@@ -458,13 +480,15 @@
             fused_kernel,
             out_shape=(made, made),
             in_specs=[pl.BlockSpec(memory_space=pltpu.SMEM)] * 3 + [whole] * 6,
-            out_specs=(vmem, vmem),
+            out_specs=(whole, whole),
             scratch_shapes=[
                 pltpu.VMEM((blocks, 2, QUARTERS, share // QUARTERS, width), jnp.bfloat16),
                 pltpu.VMEM((2, rows, width), jnp.bfloat16),
                 pltpu.VMEM((2, 2 * (rows + texts), 2 * width), jnp.bfloat16),
                 pltpu.VMEM((2 * rows, width), jnp.bfloat16),
                 pltpu.VMEM(gate_table.shape, jnp.float32),
+                pltpu.VMEM((2 * rows, features), jnp.bfloat16),
+                pltpu.SemaphoreType.DMA((blocks, 2)),
                 pltpu.SemaphoreType.DMA((blocks, QUARTERS, 5)),
                 pltpu.SemaphoreType.DMA((blocks, QUARTERS)),
                 pltpu.SemaphoreType.DMA((blocks, QUARTERS)),
@@ -473,7 +497,7 @@
                 pltpu.SemaphoreType.DMA((8,)),
             ],
             compiler_params=pltpu.CompilerParams(
-                collective_id=0, has_side_effects=True, vmem_limit_bytes=60 * 1024 * 1024
+                collective_id=0, has_side_effects=True, vmem_limit_bytes=62 * 1024 * 1024
             ),
         )(
             timesteps,

time: 53.7 us -> 52.9 us (0.985)
  Pallas kernels: 48 us -> 47.2 us
    pallas_call x1, Pallas kernels: 48 us -> 47.2 us  [fused_body(): pl.pallas_call(fused_kernel, out_shape=(made, made), in_specs=[pl.BlockSp...]
where the time goes in v3:
time: 52.9 us; the launch traced here: 52.8 us
  Pallas kernels  47.2 us (89%)
  local copies, waits for them, and re-layouts  3.02 us (6%)
  between operations  2.59 us (5%)
    pallas_call x1, Pallas kernels, fused_body(): pl.pallas_call(fused_kernel, out_shape=(made, made), in_specs=[pl.BlockSp...  47.2 us
    unnamed x4, local copies, waits for them, and re-layouts  3.02 us

profile of v3, /device:TPU:1, one launch (start us, length us, event | category | flops | bytes accessed | tf_op | source)
XLA Modules:
  0.0 52.8 jit_solution(13319874155096595132)
XLA Ops:
  2.6 47.2 %shard_map.104 = (bf16[128,3072]{1,0:T(8,128)(2,1)}, bf16[128,3072]{1,0:T(8,128)(2,1)}) custom-call(s32[1]{0:T(128)S(6)} %copy.13.timesteps, s32[1]{0:T(128)S(6)} %copy.14.image_lengths, s32[1]{0:T(128)S(6)} %copy.15.text_lengths, bf16[4,48,1536]{2,1,0:T(8,128)(2,1)} %bitcast.3, bf16[128,4608]{1,0:T(8,128)(2,1)} %image_qkv.1, bf16[128,4608]{1,0:T(8,128)(2,1)} %image_tan.1, ...), custom_call_target="tpu_custom_call" | custom-call | tf_op jit(solution)/shard_map/pallas_call | solution.py:479
  49.7 0.0 copy-start
  49.8 2.1 %copy.16 = bf16[128,3072]{1,0:T(8,128)(2,1)} copy(bf16[128,3072]{1,0:T(8,128)(2,1)} %get-tuple-element.4) | data formatting | bytes 1572864
  51.9 0.0 copy-done
  51.9 0.9 %copy.17 = bf16[128,3072]{1,0:T(8,128)(2,1)} copy(bf16[128,3072]{1,0:T(8,128)(2,1)S(1)} %copy-done) | data formatting | bytes 1572864
Async XLA Ops:
  49.7 2.1 %copy-start = (bf16[128,3072]{1,0:T(8,128)(2,1)S(1)}, bf16[128,3072]{1,0:T(8,128)(2,1)}, u32[]{:S(2)}) copy-start(bf16[128,3072]{1,0:T(8,128)(2,1)} %get-tuple-element.5) | copy-start | bytes 2359300

commit v4 on v3

--- a/solution.py
+++ b/solution.py
@@ -230,11 +230,9 @@
             act(send(block, piece, DOWN))
 
     def own_sends(act):
-        for k in range(QUARTERS):
-            piece = quarter(k)
-            if k < 2:
-                both_lines(blk, piece, act)
-            act(send(blk, piece, ACROSS))
+        act(send(blk, quarter(0), ACROSS))
+        for k in range(2):
+            both_lines(blk, quarter(k), act)
 
     def own_to_mate(act):
         for k in range(QUARTERS):
@@ -249,6 +247,8 @@
             @pl.when(j == 0)
             def _():
                 both_lines(other, piece, act)
+                for k in range(1, QUARTERS):
+                    act(send(blk, quarter(k), ACROSS))
 
             act(send(other, piece, CORE))
 

time: 52.9 us -> 52.9 us (level)
  no operation moved by 1% of the time
where the time goes in v4:
time: 52.9 us; the launch traced here: 52.7 us
  Pallas kernels  47.1 us (89%)
  local copies, waits for them, and re-layouts  3.02 us (6%)
  between operations  2.59 us (5%)
    pallas_call x1, Pallas kernels, fused_body(): pl.pallas_call(fused_kernel, out_shape=(made, made), in_specs=[pl.BlockSp...  47.1 us
    unnamed x4, local copies, waits for them, and re-layouts  3.02 us

profile of v4, /device:TPU:1, one launch (start us, length us, event | category | flops | bytes accessed | tf_op | source)
XLA Modules:
  0.0 52.7 jit_solution(4302982723936111933)
XLA Ops:
  2.6 47.1 %shard_map.104 = (bf16[128,3072]{1,0:T(8,128)(2,1)}, bf16[128,3072]{1,0:T(8,128)(2,1)}) custom-call(s32[1]{0:T(128)S(6)} %copy.13.timesteps, s32[1]{0:T(128)S(6)} %copy.14.image_lengths, s32[1]{0:T(128)S(6)} %copy.15.text_lengths, bf16[4,48,1536]{2,1,0:T(8,128)(2,1)} %bitcast.3, bf16[128,4608]{1,0:T(8,128)(2,1)} %image_qkv.1, bf16[128,4608]{1,0:T(8,128)(2,1)} %image_tan.1, ...), custom_call_target="tpu_custom_call" | custom-call | tf_op jit(solution)/shard_map/pallas_call | solution.py:479
  49.7 0.0 copy-start
  49.7 2.1 %copy.16 = bf16[128,3072]{1,0:T(8,128)(2,1)} copy(bf16[128,3072]{1,0:T(8,128)(2,1)} %get-tuple-element.4) | data formatting | bytes 1572864
  51.8 0.0 copy-done
  51.8 0.9 %copy.17 = bf16[128,3072]{1,0:T(8,128)(2,1)} copy(bf16[128,3072]{1,0:T(8,128)(2,1)S(1)} %copy-done) | data formatting | bytes 1572864
Async XLA Ops:
  49.7 2.1 %copy-start = (bf16[128,3072]{1,0:T(8,128)(2,1)S(1)}, bf16[128,3072]{1,0:T(8,128)(2,1)}, u32[]{:S(2)}) copy-start(bf16[128,3072]{1,0:T(8,128)(2,1)} %get-tuple-element.5) | copy-start | bytes 2359300
